TPU v7x, 512 devices: a whole 4x8x8 slice. The times are simulated.
512 devices in a mesh: ctx: 64 (over y_hi, z, core), head: 8 (over y_lo, x).
Axes of the slice: x: 4, y: 8 (y_hi: 4, y_lo: 2; y = y_hi * 2 + y_lo), z: 8, core: 2. Of those that a mesh axis runs over, the one named last changes fastest.
Arguments:
- queries: bfloat16 [8192, 6144], P('ctx', 'head'), may hold values from -12 to 12
- keys: bfloat16 [8192, 1024], P('ctx', 'head'), may hold values from -12 to 12
- values: bfloat16 [8192, 1024], P('ctx', 'head'), may hold values from -6 to 6
- output_cotangent: bfloat16 [8192, 6144], P('ctx', 'head'), may hold values from -3 to 3
- lengths: int32 [16], replicated, may hold values from 1 to 4096, 8192 in all
- send_order: int32 [64, 128], P('ctx'), may hold values from 0 to 127, each once within a row
Outputs:
- dq_owned: bfloat16 [8192, 6144], P('ctx', 'head')
- key_gradient_home: bfloat16 [8192, 1024], P('ctx', 'head')
- value_gradient_home: bfloat16 [8192, 1024], P('ctx', 'head')
Inputs may be any that keep to these rules, and one draw needn't show every extreme that they name: The lengths sum to 8192; the longest is exactly 4096. `send_order`: each row is a permutation of 0 to 127.
All inputs are finite; a program needn't handle non-finite values.
Results may differ from a plain program's by a relative error of at most 0.005.
Values may be sent and summed in bfloat16 or wider, within the bound.
A program may use at most 64 MiB of HBM per device.

v0:
```python
from functools import partial

import jax
import jax.numpy as jnp
from jax import lax
from jax.sharding import PartitionSpec as P

QUERY_HEADS = 48
KEY_VALUE_HEADS = 8
HEAD_SIZE = 128
SOFTCAP = 30


KEYS_PER_TILE = 512
QUERY_GROUPS = 4


def shifted(value, axis, steps):
    count = lax.axis_size(axis)
    pairs = [(source, (source + steps) % count) for source in range(count)]
    return lax.ppermute(value, axis, pairs)


def doc_starts(lengths, positions):
    starts = jnp.cumsum(lengths) - lengths
    before = positions[:, None] >= starts[None, :]
    return jnp.max(jnp.where(before, starts[None, :], 0), axis=1)


def score_tile(q_group, d_group, key_tile, value_tile, q_pos, q_start, k_pos):
    logit_scale = HEAD_SIZE ** (-0.5)
    raw_scores = (
        jnp.einsum("rngd,knd->rngk", q_group, key_tile, preferred_element_type=jnp.float32)
        * logit_scale
    )
    bent = jnp.tanh(raw_scores / SOFTCAP)
    scores = SOFTCAP * bent
    visible = (k_pos[None, :] >= q_start[:, None]) & (k_pos[None, :] <= q_pos[:, None])
    dots = jnp.einsum("rngd,knd->rngk", d_group, value_tile, preferred_element_type=jnp.float32)
    return (bent, scores, visible[:, None, None, :], dots)


def group_stats(q_group, d_group, key_tile, value_tile, q_pos, q_start, k_pos):
    bent, scores, visible, dots = score_tile(
        q_group, d_group, key_tile, value_tile, q_pos, q_start, k_pos
    )
    weights = jnp.where(visible, jnp.exp(scores), 0.0)
    return (jnp.sum(weights, axis=-1), jnp.sum(weights * dots, axis=-1))


def group_grads(q_group, d_group, key_tile, value_tile, q_pos, q_start, k_pos, log_norm, row_dots):
    bent, scores, visible, dots = score_tile(
        q_group, d_group, key_tile, value_tile, q_pos, q_start, k_pos
    )
    probability = jnp.where(visible, jnp.exp(scores - log_norm[..., None]), 0.0)
    prob_low = probability.astype(jnp.bfloat16)
    slope_grad = probability * (dots - row_dots[..., None]) * (1.0 - bent * bent)
    slope_low = slope_grad.astype(jnp.bfloat16)
    value_term = jnp.einsum("rngk,rngd->knd", prob_low, d_group, preferred_element_type=jnp.float32)
    key_term = jnp.einsum("rngk,rngd->knd", slope_low, q_group, preferred_element_type=jnp.float32)
    query_term = jnp.einsum(
        "rngk,knd->rngd", slope_low, key_tile, preferred_element_type=jnp.float32
    )
    return (query_term, key_term, value_term)


def any_visible(q_pos, q_start, k_pos):
    return jnp.any((k_pos[None, :] >= q_start[:, None]) & (k_pos[None, :] <= q_pos[:, None]))


def on_device(queries, keys, values, output_cotangent, lengths, send_order):
    ctx_size = lax.axis_size("ctx")
    my_index = lax.axis_index("ctx")
    row_count = queries.shape[0]
    per_owner = row_count // ctx_size
    kv_local = keys.shape[1] // HEAD_SIZE
    queries_per_key_head = QUERY_HEADS // KEY_VALUE_HEADS
    group_rows = row_count // QUERY_GROUPS
    logit_scale = HEAD_SIZE ** (-0.5)
    own_order = send_order[0]
    moved_q = queries[own_order].reshape(ctx_size, per_owner, queries.shape[1])
    moved_d = output_cotangent[own_order].reshape(ctx_size, per_owner, output_cotangent.shape[1])
    got_q, got_d = (
        lax.all_to_all(moved_q, "ctx", split_axis=0, concat_axis=0, tiled=True),
        lax.all_to_all(moved_d, "ctx", split_axis=0, concat_axis=0, tiled=True),
    )
    q_groups = got_q.reshape(QUERY_GROUPS, group_rows, kv_local, queries_per_key_head, HEAD_SIZE)
    d_groups = got_d.reshape(QUERY_GROUPS, group_rows, kv_local, queries_per_key_head, HEAD_SIZE)
    all_lists = lax.all_gather(send_order, "ctx", axis=0, tiled=True)
    my_lists = lax.dynamic_slice_in_dim(all_lists, my_index * per_owner, per_owner, 1)
    source_base = (jnp.arange(ctx_size, dtype=jnp.int32) * row_count)[:, None]
    q_positions = (my_lists + source_base).reshape(row_count)
    q_starts = doc_starts(lengths, q_positions)
    pos_groups = q_positions.reshape(QUERY_GROUPS, group_rows)
    start_groups = q_starts.reshape(QUERY_GROUPS, group_rows)
    all_keys, all_values = (
        lax.all_gather(keys, "ctx", axis=0, tiled=True),
        lax.all_gather(values, "ctx", axis=0, tiled=True),
    )
    key_total = all_keys.shape[0]
    key_three = all_keys.reshape(key_total, kv_local, HEAD_SIZE)
    value_three = all_values.reshape(key_total, kv_local, HEAD_SIZE)
    empty_row_stat = jnp.zeros((group_rows, kv_local, queries_per_key_head), jnp.float32)

    def stats_step(tile_index, sums_pair):
        weight_sums, weighted = sums_pair
        k_first = tile_index * KEYS_PER_TILE
        key_tile = lax.dynamic_slice_in_dim(key_three, k_first, KEYS_PER_TILE, 0)
        value_tile = lax.dynamic_slice_in_dim(value_three, k_first, KEYS_PER_TILE, 0)
        k_pos = k_first + jnp.arange(KEYS_PER_TILE, dtype=jnp.int32)
        adds_sum = []
        adds_dot = []
        for member in range(QUERY_GROUPS):
            compute = partial(
                group_stats,
                q_groups[member],
                d_groups[member],
                key_tile,
                value_tile,
                pos_groups[member],
                start_groups[member],
                k_pos,
            )
            add_sum, add_dot = lax.cond(
                any_visible(pos_groups[member], start_groups[member], k_pos),
                compute,
                lambda: (empty_row_stat, empty_row_stat),
            )
            adds_sum.append(add_sum)
            adds_dot.append(add_dot)
        return (weight_sums + jnp.stack(adds_sum), weighted + jnp.stack(adds_dot))

    stat_init = jnp.zeros((QUERY_GROUPS, group_rows, kv_local, queries_per_key_head), jnp.float32)
    weight_sums, weighted = lax.fori_loop(
        0, key_total // KEYS_PER_TILE, stats_step, (stat_init, stat_init)
    )
    log_norm = jnp.log(weight_sums)
    row_dots = weighted / weight_sums
    empty_query_gradient = jnp.zeros(
        (group_rows, kv_local, queries_per_key_head, HEAD_SIZE), jnp.float32
    )
    zero_tile = jnp.zeros((row_count, kv_local, HEAD_SIZE), jnp.float32)

    def tile_grads(key_tile, value_tile, k_pos):
        query_parts = []
        key_sum = zero_tile
        value_sum = zero_tile
        for member in range(QUERY_GROUPS):
            compute = partial(
                group_grads,
                q_groups[member],
                d_groups[member],
                key_tile,
                value_tile,
                pos_groups[member],
                start_groups[member],
                k_pos,
                log_norm[member],
                row_dots[member],
            )
            q_add, k_add, v_add = lax.cond(
                any_visible(pos_groups[member], start_groups[member], k_pos),
                compute,
                lambda: (empty_query_gradient, zero_tile, zero_tile),
            )
            query_parts.append(q_add)
            key_sum = key_sum + k_add
            value_sum = value_sum + v_add
        return (jnp.stack(query_parts), key_sum, value_sum)

    query_init = jnp.zeros(
        (QUERY_GROUPS, group_rows, kv_local, queries_per_key_head, HEAD_SIZE), jnp.float32
    )

    def cycle_one(cycle_step, running):
        key_gradient_total, value_gradient_total, query_acc = running
        block_start = jnp.mod(my_index - cycle_step, ctx_size) * row_count
        key_tile = lax.dynamic_slice_in_dim(key_three, block_start, row_count, 0)
        value_tile = lax.dynamic_slice_in_dim(value_three, block_start, row_count, 0)
        k_pos = block_start + jnp.arange(row_count, dtype=jnp.int32)
        q_add, k_add, v_add = tile_grads(key_tile, value_tile, k_pos)
        key_gradient_total, value_gradient_total = shifted(
            (key_gradient_total + k_add, value_gradient_total + v_add), "ctx", 1
        )
        return (key_gradient_total, value_gradient_total, query_acc + q_add)

    key_gradient_total, value_gradient_total, query_acc = lax.fori_loop(
        0, ctx_size, cycle_one, (zero_tile, zero_tile, query_init)
    )
    dq_owned = (query_acc * logit_scale).astype(jnp.bfloat16).reshape(row_count, queries.shape[1])
    key_gradient_home = (
        (key_gradient_total * logit_scale).astype(jnp.bfloat16).reshape(row_count, keys.shape[1])
    )
    value_gradient_home = value_gradient_total.astype(jnp.bfloat16).reshape(
        row_count, values.shape[1]
    )
    return (dq_owned, key_gradient_home, value_gradient_home)


def solution(mesh):
    return jax.shard_map(
        on_device,
        mesh=mesh,
        in_specs=(
            P("ctx", "head"),
            P("ctx", "head"),
            P("ctx", "head"),
            P("ctx", "head"),
            P(),
            P("ctx", None),
        ),
        out_specs=(P("ctx", "head"), P("ctx", "head"), P("ctx", "head")),
        check_vma=False,
    )
```

profile of v0, /device:TPU:6, one launch (start us, length us, event | category | flops | bytes accessed | tf_op | source)
XLA Modules:
  0.0 1451.4 jit_solution(15788863296969297766)
XLA Ops:
  11.0 16.6 %all-to-all-start.1 = ((bf16[64,2,768]{2,1,0:T(2,128)(2,1)}), bf16[64,2,768]{2,1,0:T(2,128)(2,1)S(1)}, u32[]{:S(2)}, u32[]{:S(2)}) async-start(bf16[64,2,768]{2,1,0:T(2,128)(2,1)} %reshape.815), calls=%async_computation.1 | async-start | bytes 393216 | tf_op jit(solution)/shard_map/all_to_all | solution.py:85
  29.2 81.8 %all-gather = s32[64,1,128]{2,1,0:T(1,128)S(1)} all-gather(s32[1,1,128]{2,1,0:T(1,128)S(1)} %bitcast.652), channel_id=1, replica_groups=mesh['ctx'=64,'head'=8] {'ctx'}, dimensions={0}, use_global_device_ids=true | all-gather | bytes 33280 | tf_op jit(solution)/shard_map/all_gather | solution.py:89
  116.9 11.9 all-to-all-done
  129.0 56.6 %all-gather.6.cloned.1.call-done = bf16[8192,128]{1,0:T(8,128)(2,1)} async-done(((bf16[128,128]{1,0:T(8,128)(2,1)}), bf16[8192,128]{1,0:T(8,128)(2,1)}) %all-gather.6.cloned.1.call-update) | async-done | bytes 2097168 | tf_op jit(solution)/shard_map/all_gather | solution.py:98
  185.6 109.3 %while.36 = (s32[]{:T(128)}, f32[4,32,1,6]{1,0,3,2:T(4,128)S(1)}, f32[4,32,1,6]{1,0,3,2:T(4,128)S(1)}, s32[4,32]{1,0:T(4,128)S(1)}, s32[4,32]{1,0:T(4,128)S(1)},...) while((s32[]{:T(128)}, f32[4,32,1,6]{1,0,3,2:T(4,128)S(1)}, ...), condition=%wide.region_23.24_spmd.clone, body=%wide.region_2.23_spmd.clone.sunk | while | flops 204151296 | bytes 5297665 | solution.py:134
  294.9 1148.2 %while.37 = (s32[]{:T(128)}, f32[128,1,128]{2,0,1:T(8,128)S(1)}, f32[128,1,128]{2,0,1:T(8,128)S(1)}, f32[4,32,1,6,128]{4,1,3,2,0:T(8,128)S(1)}, s32[]{:T(128)}, ...) while((s32[]{:T(128)}, f32[128,1,128]{2,0,1:T(8,128)S(1)}, ...), condition=%wide.region_37.38_spmd.clone, body=%wide.region_24.37_spmd.clone.sunk | while | flops 127942800 | bytes 6607694 | solution.py:187
  321.9 5.8 collective-permute-done
  339.1 6.6 collective-permute-done
  357.0 6.2 collective-permute-done
  374.5 5.8 collective-permute-done
  391.7 5.8 collective-permute-done
  408.9 5.8 collective-permute-done
  426.1 6.0 collective-permute-done
  443.3 5.8 collective-permute-done
  460.5 5.8 collective-permute-done
  477.7 5.8 collective-permute-done
  494.9 5.8 collective-permute-done
  512.1 5.8 collective-permute-done
  529.3 5.8 collective-permute-done
  546.5 5.8 collective-permute-done
  563.7 5.8 collective-permute-done
  580.9 5.8 collective-permute-done
  598.1 5.8 collective-permute-done
  615.3 5.8 collective-permute-done
  632.5 5.8 collective-permute-done
  649.7 5.8 collective-permute-done
  666.9 5.8 collective-permute-done
  684.1 5.8 collective-permute-done
  701.3 5.8 collective-permute-done
  718.5 5.8 collective-permute-done
  735.7 5.8 collective-permute-done
  752.8 5.8 collective-permute-done
  770.0 5.8 collective-permute-done
  787.2 5.8 collective-permute-done
  804.4 5.8 collective-permute-done
  821.6 5.8 collective-permute-done
  838.8 5.8 collective-permute-done
  856.0 5.8 collective-permute-done
  874.3 5.8 collective-permute-done
  892.5 5.8 collective-permute-done
  910.7 5.8 collective-permute-done
  928.9 5.8 collective-permute-done
  947.1 5.8 collective-permute-done
  965.3 5.8 collective-permute-done
  984.2 5.8 collective-permute-done
  1002.7 5.8 collective-permute-done
  1020.9 5.8 collective-permute-done
  1039.1 5.8 collective-permute-done
  1057.3 6.6 collective-permute-done
  1076.2 6.2 collective-permute-done
  1094.8 6.2 collective-permute-done
  1113.0 5.8 collective-permute-done
  1131.2 5.8 collective-permute-done
  1149.4 5.8 collective-permute-done
  1168.7 5.8 collective-permute-done
  1187.9 6.6 collective-permute-done
  1207.8 5.8 collective-permute-done
  1227.0 5.8 collective-permute-done
  1246.2 5.8 collective-permute-done
  1265.4 5.8 collective-permute-done
  1303.8 5.8 collective-permute-done
  1342.9 5.9 collective-permute-done
  1362.6 5.8 collective-permute-done
  1401.0 5.8 collective-permute-done
  (2530 shorter events, 856.1 us)
Async XLA Ops:
  7.2 121.8 %all-gather.4.cloned.1.call-start = ((), (), s32[]{:S(2)}) async-start(), calls=%async_computation.2 | async-start | bytes 2129920 | tf_op jit(solution)/shard_map/all_gather | solution.py:97
  7.9 177.6 %all-gather.6.cloned.1.call-start = ((), (), s32[]{:S(2)}) async-start(), calls=%async_computation.3 | async-start | bytes 2129920 | tf_op jit(solution)/shard_map/all_gather | solution.py:98
  11.0 100.2 %all-to-all-start.1 = ((bf16[64,2,768]{2,1,0:T(2,128)(2,1)}), bf16[64,2,768]{2,1,0:T(2,128)(2,1)S(1)}, u32[]{:S(2)}, u32[]{:S(2)}) async-start(bf16[64,2,768]{2,1,0:T(2,128)(2,1)} %reshape.815), calls=%async_computation.1 | async-start | bytes 393216 | tf_op jit(solution)/shard_map/all_to_all | solution.py:85
  111.2 17.6 %all-to-all-start = ((bf16[64,2,768]{2,1,0:T(2,128)(2,1)}), bf16[64,2,768]{2,1,0:T(2,128)(2,1)S(1)}, u32[]{:S(2)}, u32[]{:S(2)}) async-start(bf16[64,2,768]{2,1,0:T(2,128)(2,1)} %reshape.813), calls=%async_computation | async-start | bytes 393216 | tf_op jit(solution)/shard_map/all_to_all | solution.py:84
  300.4 9.8 collective-permute-start
  302.6 9.8 collective-permute-start.1
  317.9 9.8 collective-permute-start
  319.8 9.8 collective-permute-start.1
  335.1 10.6 collective-permute-start
  337.0 10.5 collective-permute-start.1
  353.0 10.2 collective-permute-start
  354.9 10.2 collective-permute-start.1
  370.5 9.8 collective-permute-start
  372.5 9.8 collective-permute-start.1
  387.7 9.8 collective-permute-start
  389.7 9.8 collective-permute-start.1
  404.9 9.8 collective-permute-start
  406.9 9.8 collective-permute-start.1
  422.1 10.0 collective-permute-start
  424.1 9.8 collective-permute-start.1
  439.3 9.8 collective-permute-start
  441.2 9.8 collective-permute-start.1
  456.5 9.8 collective-permute-start
  458.4 9.8 collective-permute-start.1
  473.7 9.8 collective-permute-start
  475.6 9.8 collective-permute-start.1
  490.9 9.8 collective-permute-start
  492.8 9.8 collective-permute-start.1
  508.1 9.8 collective-permute-start
  510.0 9.8 collective-permute-start.1
  525.3 9.8 collective-permute-start
  527.2 9.8 collective-permute-start.1
  542.5 9.8 collective-permute-start
  596.0 9.8 collective-permute-start.1
  731.6 9.8 collective-permute-start
  748.8 9.8 collective-permute-start
  800.4 9.8 collective-permute-start
  802.4 9.8 collective-permute-start.1
  817.6 9.8 collective-permute-start
  819.6 9.8 collective-permute-start.1
  945.0 9.8 collective-permute-start.1
  961.3 9.8 collective-permute-start
  963.3 10.5 collective-permute-start.1
  980.2 9.8 collective-permute-start
  982.2 10.0 collective-permute-start.1
  998.7 9.8 collective-permute-start
  1035.1 9.8 collective-permute-start
  1037.0 9.8 collective-permute-start.1
  1053.3 10.6 collective-permute-start
  1055.3 10.5 collective-permute-start.1
  1072.2 10.3 collective-permute-start
  1074.2 10.2 collective-permute-start.1
  1090.8 10.2 collective-permute-start
  1164.6 9.8 collective-permute-start
  1166.6 9.8 collective-permute-start.1
  1183.8 10.6 collective-permute-start
  1185.8 10.5 collective-permute-start.1
  1203.7 9.8 collective-permute-start
  1320.9 10.5 collective-permute-start.1
  1338.9 9.9 collective-permute-start
  1340.8 10.3 collective-permute-start.1
  1358.5 9.9 collective-permute-start
  1379.7 9.8 collective-permute-start.1
  1433.3 9.8 collective-permute-start.1
  (72 other events, 815.2 us)
Sparse Core Ops, SparseCore 0:
  11.4 88.7 all-gather.3
  103.6 81.9 all-gather.5
where the time goes:
time: 1460 us; the launch traced here: 1450 us
  waiting for transfers between devices  568 us (39%)
  starting transfers between devices  269 us (18%)
  loops' own time  219 us (15%)
  matrix products  117 us (8%)
  other arithmetic  92.3 us (6%)
  local copies, waits for them, and re-layouts  90.1 us (6%)
  blocking collectives  81.8 us (6%)
    ppermute x128, waiting for transfers between devices, shifted(): return lax.ppermute(value, axis, pairs)  498 us
    ppermute x128, starting transfers between devices, shifted(): return lax.ppermute(value, axis, pairs)  248 us
    another operation x1, loops' own time, on_device(): lax.fori_loop(0, ctx_size, cycle_one, (zero_tile, zero_tile, query_init))  165 us
    all_gather x1, blocking collectives, on_device(): all_lists = lax.all_gather(send_order, 'ctx', axis=0, tiled=True)  81.8 us
    reduce_or x80, other arithmetic, any_visible(): jnp.any((k_pos[None, :] >= q_start[:, None]) & (k_pos[None, :] <= q_pos[:...  68.4 us
    all_gather x1, waiting for transfers between devices, on_device(): lax.all_gather(values, 'ctx', axis=0, tiled=True)  56.6 us
    dynamic_slice x64, local copies, waits for them, and re-layouts, cycle_one(): lax.dynamic_slice_in_dim(value_three, block_start, row_count, 0)  50.3 us
    another operation x1, loops' own time, on_device(): lax.fori_loop(0, key_total // KEYS_PER_TILE, stats_step, (stat_init, stat...  41.4 us
  transfers between devices with their start and end apart: 132, of which 130 were waited for; matrix products, arithmetic and copies ran while one was open for 1% of the time, Pallas kernels for 0%

commit v1 on v0

v1 whole, which is shorter than its diff:
```python
import functools
import math

import jax
import jax.numpy as jnp
from jax import lax
from jax.experimental import pallas as pl
from jax.experimental.pallas import tpu as pltpu
from jax.sharding import PartitionSpec as P

HEAD_SIZE = 128
SOFTCAP = 30
TOK = 128
ROWS_Y = 4
RING = 8
UNIT = 2 * TOK
SLOTS = 3 * RING
SUM_ROWS = 16
MESH = pl.DeviceIdType.MESH
F32 = jnp.float32
BF16 = jnp.bfloat16


def dot(a, b, contract=((1,), (0,))):
    return lax.dot_general(a, b, (contract, ((), ())), preferred_element_type=F32)


def send(src, dst, send_sem, recv_sem, target):
    return pltpu.make_async_remote_copy(
        src_ref=src,
        dst_ref=dst,
        send_sem=send_sem,
        recv_sem=recv_sem,
        device_id={"ctx": target},
        device_id_type=MESH,
    )


def travels(row, way, origin, hop, core):
    if row == 0:
        if way == 0:
            return (hop <= 4) & (origin + hop <= RING - 1)
        return (hop <= 3) & (origin <= 2)
    if row == 2:
        if way == 1:
            return (hop <= 4) & (origin - hop >= 0)
        return (hop <= 3) & (origin >= 5)
    return hop <= (4 - core if way == 0 else 3 + core)


def needed(row, origin, z):
    return (row == 1) | ((row == 0) & (origin <= z)) | ((row == 2) & (origin >= z))


def kernel(
    lengths,
    order,
    queries,
    cotangent,
    keys,
    values,
    dq_out,
    dk_out,
    dv_out,
    kv,
    exps,
    slopes,
    q_t,
    d_t,
    q_scaled,
    d_scaled,
    out_acc,
    dq_acc,
    low,
    inverse,
    row_dots,
    bounds,
    part,
    sib_out,
    sib_in,
    ring_out,
    ring_in,
    y_in,
    g_ring_send,
    g_ring_recv,
    g_sib_send,
    g_sib_recv,
    g_y_send,
    g_y_recv,
    r_ring_send,
    r_ring_recv,
    r_sib_send,
    r_sib_recv,
    r_y_send,
    r_y_recv,
):
    lanes = queries.shape[1]
    heads = lanes // HEAD_SIZE
    index = lax.axis_index("ctx")
    core = lax.rem(index, 2)
    z = lax.rem(lax.div(index, 2), RING)
    h = lax.div(index, 2 * RING)
    sibling = index + 1 - 2 * core
    above = 2 * RING * h + 2 * lax.rem(z + 1, RING) + core
    below = 2 * RING * h + 2 * lax.rem(z + RING - 1, RING) + core
    toward = (above, below)
    scale = 1.0 / math.sqrt(HEAD_SIZE)

    barrier = pltpu.get_barrier_semaphore()
    for partner in (sibling, above, below):
        pl.semaphore_signal(barrier, inc=1, device_id={"ctx": partner}, device_id_type=MESH)
    for step in (-2, -1, 1, 2):

        @pl.when((h + step >= 0) & (h + step < ROWS_Y))
        def _():
            pl.semaphore_signal(
                barrier,
                inc=1,
                device_id={"ctx": index + step * 2 * RING},
                device_id_type=MESH,
            )

    own = kv.at[z, core]
    own[0] = keys[...]
    own[1] = values[...]
    pl.semaphore_wait(barrier, jnp.where((h == 1) | (h == 2), 6, 5))

    def place(row, way, distance):
        origin = lax.rem(z + RING + (distance if way else -distance), RING)
        return origin, row * RING + origin

    def gather_ring(row, way, slot):
        unit = kv.at[slot, core]
        return send(unit, unit, g_ring_send.at[way, slot], g_ring_recv.at[slot], toward[way])

    def gather_sib(slot, side):
        unit = kv.at[slot, side]
        return send(unit, unit, g_sib_send.at[slot], g_sib_recv.at[slot], sibling)

    def gather_y(step):
        return send(
            kv.at[z, core],
            kv.at[step * RING + z, core],
            g_y_send.at[step - 1],
            g_y_recv.at[step - 1],
            lax.rem(index + step * 2 * RING, 2 * RING * ROWS_Y),
        )

    def reduce_sib(slot):
        return send(sib_out.at[slot], sib_in.at[slot], r_sib_send.at[slot], r_sib_recv.at[slot], sibling)

    def reduce_ring(way, slot):
        return send(
            ring_out.at[slot],
            ring_in.at[way, slot],
            r_ring_send.at[slot],
            r_ring_recv.at[way, slot],
            toward[1 - way],
        )

    def reduce_y(step):
        return send(
            ring_out.at[step * RING + z],
            y_in.at[step - 1],
            r_y_send.at[step - 1],
            r_y_recv.at[step - 1],
            lax.rem(index + (ROWS_Y - step) * 2 * RING, 2 * RING * ROWS_Y),
        )

    for step in (1, 2):

        @pl.when(h + step < ROWS_Y)
        def _():
            gather_y(step).start()

    def arrivals(t):
        for row in range(3):
            distance = t - row

            @pl.when((distance == 0) & (h >= row))
            def _():
                if row:
                    gather_y(row).wait_recv()
                slot = row * RING + z
                for way in (0, 1):

                    @pl.when(travels(row, way, z, 1, core))
                    def _():
                        gather_ring(row, way, slot).start()

                gather_sib(slot, core).start()

            for way in (0, 1):
                origin, slot = place(row, way, distance)

                @pl.when(
                    (distance >= 1)
                    & (distance <= 4)
                    & (h >= row)
                    & travels(row, way, origin, distance, core)
                )
                def _():
                    gather_ring(row, way, slot).wait_recv()

                    @pl.when(travels(row, way, origin, distance + 1, core))
                    def _():
                        gather_ring(row, way, slot).start()

                    @pl.when(needed(row, origin, z))
                    def _():
                        gather_sib(slot, core).start()

    arrivals(0)

    for n in range(heads):
        cols = slice(n * HEAD_SIZE, (n + 1) * HEAD_SIZE)
        q_t[:, cols] = queries[:, cols].astype(F32).T.astype(BF16)
        d_t[:, cols] = cotangent[:, cols].astype(F32).T.astype(BF16)
    out_acc[...] = jnp.zeros_like(out_acc)
    dq_acc[...] = jnp.zeros_like(dq_acc)
    position = index * TOK + lax.broadcasted_iota(jnp.int32, (8, TOK), 1)
    start = jnp.zeros((8, TOK), jnp.int32)
    first = jnp.int32(0)
    for doc in range(lengths.shape[0]):
        start = jnp.where(position >= first, jnp.maximum(start, first), start)
        first = first + lengths[doc]
    bounds[0] = start
    bounds[1] = position

    def slot_of(row, way, distance):
        origin = lax.rem(z + RING + (2 * way - 1) * distance, RING)
        valid = (
            (h >= row)
            & (distance >= 0)
            & (distance <= 4)
            & needed(row, origin, z)
            & ((way == 0) | ((distance != 0) & (distance != 4)))
        )
        return origin, row * RING + origin, valid

    pairs = [slice(p * 2 * HEAD_SIZE, min((p + 1) * 2 * HEAD_SIZE, lanes)) for p in range((heads + 1) // 2)]

    def statistics(row, origin, slot):
        gather_sib(slot, 1 - core).wait_recv()
        key = kv[slot, :, 0].reshape(UNIT, HEAD_SIZE)
        value = kv[slot, :, 1].reshape(UNIT, HEAD_SIZE)
        value_t = jnp.concatenate(
            [value.astype(F32).T.astype(BF16), jnp.ones((SUM_ROWS, UNIT), BF16)], axis=0
        )
        key_at = ((h - row) * RING + origin) * UNIT + lax.broadcasted_iota(jnp.int32, (UNIT, TOK), 0)
        visible = (key_at >= bounds[0, :1]) & (key_at <= bounds[1, :1])
        for cols in pairs:
            wide = (cols.stop - cols.start) // TOK
            seen = jnp.concatenate([visible] * wide, axis=1) if wide > 1 else visible
            raw = dot(key, q_t[:, cols])
            bent = jnp.tanh(raw * (scale / SOFTCAP))
            weight = jnp.where(seen, jnp.exp2(bent * (SOFTCAP * math.log2(math.e))), 0.0)
            slopes[slot, :, cols] = weight - weight * bent * bent
            weight_low = weight.astype(BF16)
            exps[slot, :, cols] = weight_low
            out_acc[:, cols] += dot(value_t, weight_low)

    def gather_step(t, carry):
        @pl.when(t < 7)
        def _():
            arrivals(t)

        def one(q, carry):
            row, way = lax.div(q, 2), lax.rem(q, 2)
            origin, slot, valid = slot_of(row, way, t - 1 - row)

            @pl.when(valid)
            def _():
                statistics(row, origin, slot)

            return carry

        return lax.fori_loop(0, 6, one, carry)

    lax.fori_loop(1, 8, gather_step, 0)

    inverse_sum = 1.0 / out_acc[HEAD_SIZE : HEAD_SIZE + 8, :]
    inverse[...] = inverse_sum
    for n in range(heads):
        cols = slice(n * HEAD_SIZE, (n + 1) * HEAD_SIZE)
        inv = inverse_sum[:1, cols]
        d_n = d_t[:, cols].astype(F32)
        dots = jnp.sum(out_acc[:HEAD_SIZE, cols] * d_n, axis=0, keepdims=True) * inv
        row_dots[:, cols] = jnp.broadcast_to(dots, (8, HEAD_SIZE))
        d_scaled[cols, :] = (d_n * inv).T.astype(BF16)
        q_scaled[cols, :] = (q_t[:, cols].astype(F32) * inv).T.astype(BF16)

    def gradients(slot):
        key = kv[slot, :, 0].reshape(UNIT, HEAD_SIZE)
        value = kv[slot, :, 1].reshape(UNIT, HEAD_SIZE)
        key_t = key.astype(F32).T.astype(BF16)
        for cols in pairs:
            dots = dot(value, d_t[:, cols]) - row_dots[:1, cols]
            slope = (slopes[slot, :, cols] * dots).astype(BF16)
            low[:, cols] = slope
            dq_acc[:, cols] += dot(key_t, slope)
        key_part = dot(low[...], q_scaled[...])
        value_part = dot(exps[slot], d_scaled[...])
        for side in (0, 1):
            rows = slice(side * TOK, (side + 1) * TOK)

            @pl.when(core == side)
            def _():
                part[slot, 0] = key_part[rows]
                part[slot, 1] = value_part[rows]

            @pl.when(core != side)
            def _():
                sib_out[slot, 0] = key_part[rows].astype(BF16)
                sib_out[slot, 1] = value_part[rows].astype(BF16)

        reduce_sib(slot).start()

    def combine(u):
        for row in (2, 1, 0):
            distance = 5 - u + (2 - row)
            for way in (0, 1):
                origin, slot = place(row, way, distance)

                @pl.when(
                    (distance >= 1)
                    & (distance <= 4)
                    & (h >= row)
                    & travels(row, way, origin, distance, core)
                )
                def _():
                    @pl.when(needed(row, origin, z))
                    def _():
                        reduce_sib(slot).wait_recv()
                        part[slot] = part[slot] + sib_in[slot].astype(F32)

                    @pl.when(jnp.logical_not(needed(row, origin, z)))
                    def _():
                        part[slot] = jnp.zeros(part.shape[1:], F32)

                    @pl.when(travels(row, way, origin, distance + 1, core))
                    def _():
                        reduce_ring(way, slot).wait_recv()
                        part[slot] = part[slot] + ring_in[way, slot].astype(F32)

                    ring_out[slot] = part[slot].astype(BF16)
                    reduce_ring(way, slot).start()

            @pl.when((distance == 0) & (h >= row))
            def _():
                slot = row * RING + z
                reduce_sib(slot).wait_recv()
                part[slot] = part[slot] + sib_in[slot].astype(F32)
                for way in (0, 1):

                    @pl.when(travels(row, way, z, 1, core))
                    def _():
                        reduce_ring(way, slot).wait_recv()
                        part[slot] = part[slot] + ring_in[way, slot].astype(F32)

                if row:
                    ring_out[slot] = part[slot].astype(BF16)
                    reduce_y(row).start()

    def reduce_step(u, carry):
        def one(q, carry):
            row, way = 2 - lax.div(q, 2), lax.rem(q, 2)
            _, slot, valid = slot_of(row, way, 6 - u - row)

            @pl.when(valid)
            def _():
                gradients(slot)

            return carry

        carry = lax.fori_loop(0, 6, one, carry)
        combine(u)
        return carry

    lax.fori_loop(0, 8, reduce_step, 0)

    picked = (lax.broadcasted_iota(jnp.int32, (TOK, TOK), 0) == order[...]).astype(F32).T.astype(BF16)
    for n in range(heads):
        cols = slice(n * HEAD_SIZE, (n + 1) * HEAD_SIZE)
        grad_t = (dq_acc[:, cols] * (inverse[:1, cols] * scale)).astype(BF16)
        dq_out[:, cols] = dot(picked, grad_t, ((1,), (1,))).astype(BF16)

    for step in (1, 2):

        @pl.when(h + step < ROWS_Y)
        def _():
            reduce_y(step).wait_recv()
            part[z] = part[z] + y_in[step - 1].astype(F32)

    dk_out[...] = (part[z, 0] * scale).astype(BF16)
    dv_out[...] = part[z, 1].astype(BF16)

    for step in (1, 2):

        @pl.when(h + step < ROWS_Y)
        def _():
            gather_y(step).wait_send()

        @pl.when(h >= step)
        def _():
            reduce_y(step).wait_send()

    def drain(distance, carry):
        for row in range(3):
            for way in (0, 1):
                origin, slot = place(row, way, distance)

                @pl.when((h >= row) & travels(row, way, origin, distance + 1, core))
                def _():
                    gather_ring(row, way, slot).wait_send()

                @pl.when(
                    (distance >= 1) & (h >= row) & travels(row, way, origin, distance, core)
                )
                def _():
                    reduce_ring(way, slot).wait_send()

                _, _, valid = slot_of(row, way, distance)

                @pl.when(valid)
                def _():
                    gather_sib(slot, core).wait_send()
                    reduce_sib(slot).wait_send()

        return carry

    lax.fori_loop(0, 5, drain, 0)


def run_kernel(queries, cotangent, keys, values, lengths, order):
    lanes = queries.shape[1]
    vmem = pl.BlockSpec(memory_space=pltpu.VMEM)
    block = (2, TOK, HEAD_SIZE)
    dma = pltpu.SemaphoreType.DMA
    return pl.pallas_call(
        kernel,
        out_shape=(
            jax.ShapeDtypeStruct((TOK, lanes), BF16),
            jax.ShapeDtypeStruct((TOK, HEAD_SIZE), BF16),
            jax.ShapeDtypeStruct((TOK, HEAD_SIZE), BF16),
        ),
        in_specs=[pl.BlockSpec(memory_space=pltpu.SMEM)] + [vmem] * 5,
        out_specs=(vmem, vmem, vmem),
        scratch_shapes=[
            pltpu.VMEM((SLOTS, 2) + block, BF16),
            pltpu.VMEM((SLOTS, UNIT, lanes), BF16),
            pltpu.VMEM((SLOTS, UNIT, lanes), F32),
            pltpu.VMEM((HEAD_SIZE, lanes), BF16),
            pltpu.VMEM((HEAD_SIZE, lanes), BF16),
            pltpu.VMEM((lanes, HEAD_SIZE), BF16),
            pltpu.VMEM((lanes, HEAD_SIZE), BF16),
            pltpu.VMEM((HEAD_SIZE + SUM_ROWS, lanes), F32),
            pltpu.VMEM((HEAD_SIZE, lanes), F32),
            pltpu.VMEM((UNIT, lanes), BF16),
            pltpu.VMEM((8, lanes), F32),
            pltpu.VMEM((8, lanes), F32),
            pltpu.VMEM((2, 8, TOK), jnp.int32),
            pltpu.VMEM((SLOTS,) + block, F32),
            pltpu.VMEM((SLOTS,) + block, BF16),
            pltpu.VMEM((SLOTS,) + block, BF16),
            pltpu.VMEM((SLOTS,) + block, BF16),
            pltpu.VMEM((2, SLOTS) + block, BF16),
            pltpu.VMEM((2,) + block, BF16),
            dma((2, SLOTS)),
            dma((SLOTS,)),
            dma((SLOTS,)),
            dma((SLOTS,)),
            dma((2,)),
            dma((2,)),
            dma((SLOTS,)),
            dma((2, SLOTS)),
            dma((SLOTS,)),
            dma((SLOTS,)),
            dma((2,)),
            dma((2,)),
        ],
        compiler_params=pltpu.CompilerParams(
            collective_id=0, has_side_effects=True, vmem_limit_bytes=58 * 1024 * 1024
        ),
        name="attention_backward",
    )(lengths, order, queries, cotangent, keys, values)


def on_device(queries, keys, values, output_cotangent, lengths, send_order):
    rows, lanes = queries.shape
    dq, dk, dv = run_kernel(queries, output_cotangent, keys, values, lengths, send_order)
    owners = lax.axis_size("ctx")
    moved = dq.reshape(owners, rows // owners, lanes)
    dq_owned = lax.all_to_all(moved, "ctx", split_axis=0, concat_axis=0, tiled=True)
    return dq_owned.reshape(rows, lanes), dk, dv


def solution(mesh):
    return jax.shard_map(
        on_device,
        mesh=mesh,
        in_specs=(
            P("ctx", "head"),
            P("ctx", "head"),
            P("ctx", "head"),
            P("ctx", "head"),
            P(),
            P("ctx", None),
        ),
        out_specs=(P("ctx", "head"), P("ctx", "head"), P("ctx", "head")),
        check_vma=False,
    )
```

time: 1460 us -> 107 us (0.07)
  waiting for transfers between devices: 568 us -> 13 us
  starting transfers between devices: 269 us -> 15.7 us
  loops' own time: 219 us -> 0 us
  matrix products: 117 us -> 0 us
  other arithmetic: 92.3 us -> 0 us
  local copies, waits for them, and re-layouts: 90.1 us -> 3.82 us
  blocking collectives: 81.8 us -> 0 us
  Pallas kernels: 0 us -> 72.8 us
    ppermute x128 -> x0, waiting for transfers between devices: 498 us -> none  [shifted(): return lax.ppermute(value, axis, pairs)]
    ppermute x128 -> x0, starting transfers between devices: 248 us -> none  [shifted(): return lax.ppermute(value, axis, pairs)]
    another operation x322 -> x0, loops' own time: 219 us -> none  [the longest x1 165 us: on_device(): lax.fori_loop(0, ctx_size, cycle_one, (zero_tile, zero_tile, query_init))]
    dot_general x586 -> x0, matrix products: 117 us -> none  [the longest x106 28.3 us: group_grads(): jnp.einsum('rngk,rngd->knd', prob_low, d_group, preferred_element_type=jn...]
    all_gather x1 -> x0, blocking collectives: 81.8 us -> none  [on_device(): all_lists = lax.all_gather(send_order, 'ctx', axis=0, tiled=True)]
    dynamic_slice x98 -> x0, local copies, waits for them, and re-layouts: 79.9 us -> none  [the longest x64 50.3 us: cycle_one(): lax.dynamic_slice_in_dim(value_three, block_start, row_count, 0)]
    pallas_call x0 -> x1, Pallas kernels: none -> 72.8 us  [run_kernel(): pl.pallas_call(kernel, out_shape=(jax.ShapeDtypeStruct((TOK, lanes), BF16...]
    reduce_or x80 -> x0, other arithmetic: 68.4 us -> none  [any_visible(): jnp.any((k_pos[None, :] >= q_start[:, None]) & (k_pos[None, :] <= q_pos[:...]
  transfers between devices with their start and end apart: 132 -> 1, of which waited for: 130 -> 1; matrix products, arithmetic and copies ran while one was open for 1% -> 0% of each run, Pallas kernels for 0% -> 0%
where the time goes in v1:
time: 107 us; the launch traced here: 106 us
  Pallas kernels  72.8 us (68%)
  starting transfers between devices  15.7 us (15%)
  waiting for transfers between devices  13 us (12%)
  local copies, waits for them, and re-layouts  3.82 us (4%)
    pallas_call x1, Pallas kernels, run_kernel(): pl.pallas_call(kernel, out_shape=(jax.ShapeDtypeStruct((TOK, lanes), BF16...  72.8 us
    all_to_all x1, starting transfers between devices, on_device(): lax.all_to_all(moved, 'ctx', split_axis=0, concat_axis=0, tiled=True)  15.7 us
    all_to_all x1, waiting for transfers between devices, on_device(): lax.all_to_all(moved, 'ctx', split_axis=0, concat_axis=0, tiled=True)  13 us
  transfers between devices with their start and end apart: 1, of which 1 were waited for; matrix products, arithmetic and copies ran while one was open for 0% of the time, Pallas kernels for 0%

profile of v1, /device:TPU:6, one launch (start us, length us, event | category | flops | bytes accessed | tf_op | source)
XLA Modules:
  0.0 105.9 jit_solution(3057554125396019754)
XLA Ops:
  0.6 72.8 %attention_backward.1 = (bf16[128,768]{1,0:T(8,128)(2,1)}, bf16[128,128]{1,0:T(8,128)(2,1)}, bf16[128,128]{1,0:T(8,128)(2,1)}) custom-call(s32[16]{0:T(128)} %lengths.1, s32[1,128]{1,0:T(1,128)} %order.1, bf16[128,768]{1,0:T(8,128)(2,1)} %queries.1, bf16[128,768]{1,0:T(8,128)(2,1)} %cotangent.1, bf16[128,128]{1,0:T(8,128)(2,1)} %keys.1, bf16[128,128]{1,0:T(8,128)(2,1)} %values.1), custom_call_target="tpu_custom_call" | custom-call | tf_op jit(solution)/shard_map/attention_backward/pallas_call | solution.py:440
  73.4 1.7 %reshape.12 = bf16[64,2,768]{2,1,0:T(2,128)(2,1)} reshape(bf16[128,768]{1,0:T(8,128)(2,1)} %get-tuple-element.6) | data formatting | bytes 393216 | tf_op jit(solution)/shard_map/reshape | solution.py:493
  75.1 15.7 %all-to-all-start = ((bf16[64,2,768]{2,1,0:T(2,128)(2,1)}), bf16[64,2,768]{2,1,0:T(2,128)(2,1)S(1)}, u32[]{:S(2)}, u32[]{:S(2)}) async-start(bf16[64,2,768]{2,1,0:T(2,128)(2,1)} %reshape.12), calls=%async_computation | async-start | bytes 393216 | tf_op jit(solution)/shard_map/all_to_all | solution.py:494
  90.8 0.0 copy-start.1
  90.8 13.0 %all-to-all-done = bf16[64,2,768]{2,1,0:T(2,128)(2,1)S(1)} async-done(((bf16[64,2,768]{2,1,0:T(2,128)(2,1)}), bf16[64,2,768]{2,1,0:T(2,128)(2,1)S(1)}, u32[]{:S(2)}, u32[]{:S(2)}) %all-to-all-start) | async-done | bytes 196640 | tf_op jit(solution)/shard_map/all_to_all | solution.py:494
  103.8 0.8 reshape.13
  104.5 0.0 copy-done.1
  104.5 0.0 copy-start
  104.5 0.6 copy.11
  105.2 0.2 copy-done
  105.3 0.6 copy.12
Async XLA Ops:
  75.1 28.7 %all-to-all-start = ((bf16[64,2,768]{2,1,0:T(2,128)(2,1)}), bf16[64,2,768]{2,1,0:T(2,128)(2,1)S(1)}, u32[]{:S(2)}, u32[]{:S(2)}) async-start(bf16[64,2,768]{2,1,0:T(2,128)(2,1)} %reshape.12), calls=%async_computation | async-start | bytes 393216 | tf_op jit(solution)/shard_map/all_to_all | solution.py:494
  90.8 13.7 %copy-start.1 = (bf16[128,128]{1,0:T(8,128)(2,1)S(1)}, bf16[128,128]{1,0:T(8,128)(2,1)}, u32[]{:S(2)}) copy-start(bf16[128,128]{1,0:T(8,128)(2,1)} %get-tuple-element.13) | copy-start | bytes 98308
  104.5 0.8 copy-start

commit v2 on v1

v2 whole, which is shorter than its diff:
```python
import functools
import math

import jax
import jax.numpy as jnp
from jax import lax
from jax.experimental import pallas as pl
from jax.experimental.pallas import tpu as pltpu
from jax.sharding import PartitionSpec as P

HEAD_SIZE = 128
SOFTCAP = 30
TOK = 128
ROWS_Y = 4
RING = 8
UNIT = 2 * TOK
SLOTS = 3 * RING
SUM_ROWS = 16
HELD = 17
PAD = 8
GATHER_ORDER = ((0, 0), (1, 0), (0, 1), (2, 0), (1, 1), (2, 1), (0, 2), (1, 2), (2, 2))
REDUCE_ORDER = ((2, 2), (1, 2), (0, 2), (2, 1), (1, 1), (0, 1), (2, 0), (1, 0), (0, 0))
STAGES = ((), (2, -2, 1, -1), (3, -3, 4, -4))
PORT = {1: 0, 2: 1, -1: 2, -2: 3, 3: 4, 4: 5, -3: 6, -4: 7}
MESH = pl.DeviceIdType.MESH
F32 = jnp.float32
BF16 = jnp.bfloat16


def dot(a, b, contract=((1,), (0,))):
    return lax.dot_general(a, b, (contract, ((), ())), preferred_element_type=F32)


def send(src, dst, send_sem, recv_sem, target):
    return pltpu.make_async_remote_copy(
        src_ref=src,
        dst_ref=dst,
        send_sem=send_sem,
        recv_sem=recv_sem,
        device_id={"ctx": target},
        device_id_type=MESH,
    )


def needed(row, origin, z):
    return (row == 1) | ((row == 0) & (origin <= z)) | ((row == 2) & (origin >= z))


def reaches(row, origin, shift, core):
    z = lax.rem(origin + shift + RING, RING)
    if abs(shift) == 4:
        if row == 1:
            return core == (0 if shift > 0 else 1)
        return needed(row, origin, z) & ((row == 0) == (shift > 0))
    wanted = needed(row, origin, z)
    if abs(shift) == 2:
        for further in (3, 4):
            wanted = wanted | reaches(row, origin, further if shift > 0 else -further, core)
    return wanted


def pick(index, table):
    value = jnp.int32(table[0])
    for i in range(1, len(table)):
        value = jnp.where(index == i, table[i], value)
    return value


def kernel(
    lengths,
    order,
    queries,
    cotangent,
    keys,
    values,
    dq_out,
    dk_out,
    dv_out,
    kv,
    exps,
    slopes,
    q_t,
    d_t,
    q_rows,
    d_rows,
    out_acc,
    dq_acc,
    low_slope,
    low_prob,
    inverse,
    row_dots,
    bounds,
    spread,
    part,
    sib_out,
    sib_in,
    ring_out,
    ring_in,
    y_in,
    rows_out,
    rows_in,
    g_ring_send,
    g_ring_recv,
    g_sib_send,
    g_sib_recv,
    g_y_send,
    g_y_recv,
    r_ring_send,
    r_ring_recv,
    r_sib_send,
    r_sib_recv,
    r_y_send,
    r_y_recv,
    rows_send,
    rows_recv,
    ready,
):
    lanes = queries.shape[1]
    heads = lanes // HEAD_SIZE
    devices = 2 * RING * ROWS_Y
    index = lax.axis_index("ctx")
    core = lax.rem(index, 2)
    z = lax.rem(lax.div(index, 2), RING)
    h = lax.div(index, 2 * RING)
    sibling = index + 1 - 2 * core
    scale = 1.0 / math.sqrt(HEAD_SIZE)

    def along(place):
        return 2 * RING * h + 2 * lax.rem(place + RING, RING) + core

    barrier = pltpu.get_barrier_semaphore()
    ring_mates = [along(z + step) for step in range(1, RING)]
    column_mates = [
        lax.rem(index - core + 2 * RING * step + lax.rem(core + side, 2), devices)
        for step in range(ROWS_Y)
        for side in (0, 1)
        if step or side
    ]
    for mate in ring_mates + column_mates:
        pl.semaphore_signal(barrier, inc=1, device_id={"ctx": mate}, device_id_type=MESH)

    own = kv.at[z, core]
    own[0] = keys[...]
    own[1] = values[...]
    pl.semaphore_wait(barrier, len(ring_mates + column_mates))

    def gather_ring(row, origin, shift):
        unit = kv.at[row * RING + origin, core]
        return send(
            unit,
            unit,
            g_ring_send.at[row, PORT[shift]],
            g_ring_recv.at[row * RING + origin],
            along(origin + shift),
        )

    def gather_sib(slot, side):
        unit = kv.at[slot, side]
        return send(unit, unit, g_sib_send.at[slot], g_sib_recv.at[slot], sibling)

    def gather_y(step):
        return send(
            kv.at[z, core],
            kv.at[step * RING + z, core],
            g_y_send.at[step - 1],
            g_y_recv.at[step - 1],
            lax.rem(index + step * 2 * RING, devices),
        )

    def reduce_sib(slot):
        return send(sib_out.at[slot], sib_in.at[slot], r_sib_send.at[slot], r_sib_recv.at[slot], sibling)

    def reduce_ring(row, origin, shift):
        stop = 0 if abs(shift) <= 2 else (2 if shift > 0 else -2)
        return send(
            ring_out.at[row * RING + origin],
            ring_in.at[row, PORT[shift]],
            r_ring_send.at[row * RING + origin],
            r_ring_recv.at[row, PORT[shift]],
            along(origin + stop),
        )

    def reduce_y(step):
        return send(
            ring_out.at[step * RING + z],
            y_in.at[step - 1],
            r_y_send.at[step - 1],
            r_y_recv.at[step - 1],
            lax.rem(index + (ROWS_Y - step) * 2 * RING, devices),
        )

    for step in (1, 2):

        @pl.when(h + step < ROWS_Y)
        def _():
            gather_y(step).start()

    def origin_of(shift):
        return lax.rem(z - shift + RING, RING)

    def further_of(shift):
        if abs(shift) != 2:
            return ()
        return (3, 4) if shift > 0 else (-3, -4)

    def arrive(row, stage):
        if stage == 0:
            if row:
                gather_y(row).wait_recv()
            for shift in (2, -2, 1, -1):

                @pl.when(reaches(row, z, shift, core))
                def _():
                    gather_ring(row, z, shift).start()

            gather_sib(row * RING + z, core).start()
        for shift in STAGES[stage]:
            origin = origin_of(shift)

            @pl.when(reaches(row, origin, shift, core))
            def _():
                gather_ring(row, origin, shift).wait_recv()
                for further in further_of(shift):

                    @pl.when(reaches(row, origin, further, core))
                    def _():
                        gather_ring(row, origin, further).start()

                @pl.when(needed(row, origin, z))
                def _():
                    gather_sib(row * RING + origin, core).start()

    arrive(*GATHER_ORDER[0])
    for mate in column_mates:
        pl.semaphore_signal(ready, inc=1, device_id={"ctx": mate}, device_id_type=MESH)

    for n in range(heads):
        cols = slice(n * HEAD_SIZE, (n + 1) * HEAD_SIZE)
        q_t[:, cols] = queries[:, cols].astype(F32).T.astype(BF16)
        d_t[:, cols] = cotangent[:, cols].astype(F32).T.astype(BF16)
        q_rows[cols, :] = queries[:, cols]
        d_rows[cols, :] = cotangent[:, cols]
    out_acc[...] = jnp.zeros_like(out_acc)
    dq_acc[...] = jnp.zeros_like(dq_acc)
    position = index * TOK + lax.broadcasted_iota(jnp.int32, (8, TOK), 1)
    start = jnp.zeros((8, TOK), jnp.int32)
    first = jnp.int32(0)
    for doc in range(lengths.shape[0]):
        start = jnp.where(position >= first, jnp.maximum(start, first), start)
        first = first + lengths[doc]
    bounds[0] = start
    bounds[1] = position

    picked = (lax.broadcasted_iota(jnp.int32, (TOK, TOK), 0) == order[...]).astype(F32).T.astype(BF16)
    target = lax.broadcasted_iota(jnp.int32, (TOK * PAD, TOK), 0)
    source = PAD * lax.broadcasted_iota(jnp.int32, (TOK * PAD, TOK), 1)
    for n in range(heads):
        place = (target == source + n).astype(F32).astype(BF16)
        spread[:, n * HEAD_SIZE : (n + 1) * HEAD_SIZE] = dot(place, picked).astype(BF16)

    def member(row, stage, i):
        distance = jnp.where(stage == 0, 0, 2 * stage - 1 + lax.div(i, 2))
        origin = lax.rem(z + RING + (2 * lax.rem(i, 2) - 1) * distance, RING)
        count = jnp.where(stage == 0, 1, jnp.where(stage == 1, 4, 3))
        valid = (h >= row) & needed(row, origin, z) & (i < count)
        kept = jnp.where(row == 1, RING + origin, jnp.where((row == 2) & (origin == z), 2 * RING, origin))
        return origin, row * RING + origin, kept, valid

    def statistics(row, origin, slot, kept):
        gather_sib(slot, 1 - core).wait_recv()
        key = kv[slot, :, 0].reshape(UNIT, HEAD_SIZE)
        value = kv[slot, :, 1].reshape(UNIT, HEAD_SIZE)
        value_t = jnp.concatenate(
            [value.astype(F32).T.astype(BF16), jnp.ones((SUM_ROWS, UNIT), BF16)], axis=0
        )
        key_at = ((h - row) * RING + origin) * UNIT + lax.broadcasted_iota(jnp.int32, (UNIT, TOK), 0)
        visible = (key_at >= bounds[0, :1]) & (key_at <= bounds[1, :1])
        seen = jnp.concatenate([visible] * heads, axis=1)
        bent = jnp.tanh(dot(key, q_t[...]) * (scale / SOFTCAP))
        weight = jnp.where(seen, jnp.exp2(bent * (SOFTCAP * math.log2(math.e))), 0.0)
        exps[kept] = weight
        slopes[kept] = weight - weight * bent * bent
        out_acc[...] += dot(value_t, weight.astype(BF16))

    def gather_step(g, carry):
        for i in range(1, len(GATHER_ORDER)):

            @pl.when((g == i) & (h >= GATHER_ORDER[i][0]))
            def _():
                arrive(*GATHER_ORDER[i])

        row = pick(g - 1, [r for r, _ in GATHER_ORDER])
        stage = pick(g - 1, [s for _, s in GATHER_ORDER])

        def one(i, carry):
            origin, slot, kept, valid = member(row, stage, i)

            @pl.when(valid)
            def _():
                statistics(row, origin, slot, kept)

            return carry

        return lax.fori_loop(0, 4, one, carry)

    lax.fori_loop(1, len(GATHER_ORDER) + 1, gather_step, 0)

    inverse_sum = 1.0 / out_acc[HEAD_SIZE : HEAD_SIZE + 8, :]
    inverse[...] = inverse_sum
    dots = jnp.sum(out_acc[:HEAD_SIZE, :] * d_t[...].astype(F32), axis=0, keepdims=True)
    row_dots[...] = dots * inverse_sum

    def gradients(slot, kept):
        key = kv[slot, :, 0].reshape(UNIT, HEAD_SIZE)
        value = kv[slot, :, 1].reshape(UNIT, HEAD_SIZE)
        key_t = key.astype(F32).T.astype(BF16)
        inv = inverse[:1, :]
        dots = (dot(value, d_t[...]) - row_dots[:1, :]) * inv
        slope = (slopes[kept] * dots).astype(BF16)
        low_slope[...] = slope
        low_prob[...] = (exps[kept] * inv).astype(BF16)
        dq_acc[...] += dot(key_t, slope)
        key_part = dot(low_slope[...], q_rows[...])
        value_part = dot(low_prob[...], d_rows[...])
        for side in (0, 1):
            rows = slice(side * TOK, (side + 1) * TOK)

            @pl.when(core == side)
            def _():
                part[slot, 0] = key_part[rows]
                part[slot, 1] = value_part[rows]

            @pl.when(core != side)
            def _():
                sib_out[slot, 0] = key_part[rows].astype(BF16)
                sib_out[slot, 1] = value_part[rows].astype(BF16)

        reduce_sib(slot).start()

    def combine(row, stage):
        if stage == 0:
            slot = row * RING + z
            reduce_sib(slot).wait_recv()
            part[slot] = part[slot] + sib_in[slot].astype(F32)
            for shift in (1, -1, 2, -2):

                @pl.when(reaches(row, z, shift, core))
                def _():
                    reduce_ring(row, z, shift).wait_recv()
                    part[slot] = part[slot] + ring_in[row, PORT[shift]].astype(F32)

            if row:
                ring_out[slot] = part[slot].astype(BF16)
                reduce_y(row).start()
        for shift in STAGES[stage]:
            origin = origin_of(shift)
            slot = row * RING + origin

            @pl.when(reaches(row, origin, shift, core))
            def _():
                if stage == 1:

                    @pl.when(jnp.logical_not(needed(row, origin, z)))
                    def _():
                        part[slot] = jnp.zeros(part.shape[1:], F32)

                @pl.when(needed(row, origin, z))
                def _():
                    reduce_sib(slot).wait_recv()
                    part[slot] = part[slot] + sib_in[slot].astype(F32)

                for further in further_of(shift):

                    @pl.when(reaches(row, origin, further, core))
                    def _():
                        reduce_ring(row, origin, further).wait_recv()
                        part[slot] = part[slot] + ring_in[row, PORT[further]].astype(F32)

                ring_out[slot] = part[slot].astype(BF16)
                reduce_ring(row, origin, shift).start()

    def reduce_step(g, carry):
        row = pick(g, [r for r, _ in REDUCE_ORDER])
        stage = pick(g, [s for _, s in REDUCE_ORDER])

        def one(i, carry):
            _, slot, kept, valid = member(row, stage, i)

            @pl.when(valid)
            def _():
                gradients(slot, kept)

            return carry

        carry = lax.fori_loop(0, 4, one, carry)
        for i in range(len(REDUCE_ORDER) - 1):

            @pl.when((g == i + 1) & (h >= REDUCE_ORDER[i][0]))
            def _():
                combine(*REDUCE_ORDER[i])

        return carry

    lax.fori_loop(0, len(REDUCE_ORDER), reduce_step, 0)

    grad_t = (dq_acc[...] * scale).astype(BF16)
    moved = dot(spread[...], grad_t, ((1,), (1,))).astype(BF16)
    rows_out[...] = moved.reshape(rows_out.shape)

    pl.semaphore_wait(ready, len(column_mates))

    def rows_to(step, carry):
        owner = lax.rem(index + step, devices)
        send(rows_out.at[owner], rows_in.at[index], rows_send, rows_recv, owner).start()
        return carry

    lax.fori_loop(1, devices, rows_to, 0)
    rows_in[index] = rows_out[index]

    combine(*REDUCE_ORDER[-1])
    for step in (1, 2):

        @pl.when(h + step < ROWS_Y)
        def _():
            reduce_y(step).wait_recv()
            part[z] = part[z] + y_in[step - 1].astype(F32)

    dk_out[...] = (part[z, 0] * scale).astype(BF16)
    dv_out[...] = part[z, 1].astype(BF16)

    for step in (1, 2):

        @pl.when(h + step < ROWS_Y)
        def _():
            gather_y(step).wait_send()

        @pl.when(h >= step)
        def _():
            reduce_y(step).wait_send()

    for row in range(3):

        @pl.when(h >= row)
        def _():
            gather_sib(row * RING + z, core).wait_send()
            reduce_sib(row * RING + z).wait_send()
            for shift in PORT:
                origin = origin_of(shift)
                if abs(shift) <= 2:

                    @pl.when(reaches(row, z, shift, core))
                    def _():
                        gather_ring(row, z, shift).wait_send()

                for further in further_of(shift):

                    @pl.when(reaches(row, origin, further, core))
                    def _():
                        gather_ring(row, origin, further).wait_send()

                @pl.when(reaches(row, origin, shift, core))
                def _():
                    reduce_ring(row, origin, shift).wait_send()

                    @pl.when(needed(row, origin, z))
                    def _():
                        gather_sib(row * RING + origin, core).wait_send()
                        reduce_sib(row * RING + origin).wait_send()

    others = pl.ds(0, devices - 1)
    everyone = send(rows_out.at[others], rows_in.at[others], rows_send, rows_recv, sibling)
    everyone.wait_recv()
    everyone.wait_send()
    dq_out[...] = rows_in[...]


def run_kernel(queries, cotangent, keys, values, lengths, order):
    lanes = queries.shape[1]
    devices = lax.axis_size("ctx")
    vmem = pl.BlockSpec(memory_space=pltpu.VMEM)
    block = (2, TOK, HEAD_SIZE)
    travelling = (devices, TOK // devices * PAD, HEAD_SIZE)
    dma = pltpu.SemaphoreType.DMA
    return pl.pallas_call(
        kernel,
        out_shape=(
            jax.ShapeDtypeStruct(travelling, BF16),
            jax.ShapeDtypeStruct((TOK, HEAD_SIZE), BF16),
            jax.ShapeDtypeStruct((TOK, HEAD_SIZE), BF16),
        ),
        in_specs=[pl.BlockSpec(memory_space=pltpu.SMEM)] + [vmem] * 5,
        out_specs=(vmem, vmem, vmem),
        scratch_shapes=[
            pltpu.VMEM((SLOTS, 2) + block, BF16),
            pltpu.VMEM((HELD, UNIT, lanes), F32),
            pltpu.VMEM((HELD, UNIT, lanes), F32),
            pltpu.VMEM((HEAD_SIZE, lanes), BF16),
            pltpu.VMEM((HEAD_SIZE, lanes), BF16),
            pltpu.VMEM((lanes, HEAD_SIZE), BF16),
            pltpu.VMEM((lanes, HEAD_SIZE), BF16),
            pltpu.VMEM((HEAD_SIZE + SUM_ROWS, lanes), F32),
            pltpu.VMEM((HEAD_SIZE, lanes), F32),
            pltpu.VMEM((UNIT, lanes), BF16),
            pltpu.VMEM((UNIT, lanes), BF16),
            pltpu.VMEM((8, lanes), F32),
            pltpu.VMEM((8, lanes), F32),
            pltpu.VMEM((2, 8, TOK), jnp.int32),
            pltpu.VMEM((TOK * PAD, lanes), BF16),
            pltpu.VMEM((SLOTS,) + block, F32),
            pltpu.VMEM((SLOTS,) + block, BF16),
            pltpu.VMEM((SLOTS,) + block, BF16),
            pltpu.VMEM((SLOTS,) + block, BF16),
            pltpu.VMEM((3, len(PORT)) + block, BF16),
            pltpu.VMEM((2,) + block, BF16),
            pltpu.VMEM(travelling, BF16),
            pltpu.VMEM(travelling, BF16),
            dma((3, len(PORT))),
            dma((SLOTS,)),
            dma((SLOTS,)),
            dma((SLOTS,)),
            dma((2,)),
            dma((2,)),
            dma((SLOTS,)),
            dma((3, len(PORT))),
            dma((SLOTS,)),
            dma((SLOTS,)),
            dma((2,)),
            dma((2,)),
            dma,
            dma,
            pltpu.SemaphoreType.REGULAR,
        ],
        compiler_params=pltpu.CompilerParams(
            collective_id=0, has_side_effects=True, vmem_limit_bytes=58 * 1024 * 1024
        ),
        name="attention_backward",
    )(lengths, order, queries, cotangent, keys, values)


def on_device(queries, keys, values, output_cotangent, lengths, send_order):
    rows, lanes = queries.shape
    moved, dk, dv = run_kernel(queries, output_cotangent, keys, values, lengths, send_order)
    dq_owned = moved.reshape(rows, PAD, HEAD_SIZE)[:, : lanes // HEAD_SIZE]
    return dq_owned.reshape(rows, lanes), dk, dv


def solution(mesh):
    return jax.shard_map(
        on_device,
        mesh=mesh,
        in_specs=(
            P("ctx", "head"),
            P("ctx", "head"),
            P("ctx", "head"),
            P("ctx", "head"),
            P(),
            P("ctx", None),
        ),
        out_specs=(P("ctx", "head"), P("ctx", "head"), P("ctx", "head")),
        check_vma=False,
    )
```

time: 107 us -> 81.3 us (0.76)
  the two profiles are of different devices: /device:TPU:6 before, /device:TPU:13 now
where the time goes in v2:
time: 81.3 us; the launch traced here: 81.1 us
  Pallas kernels  77.1 us (95%)
  local copies, waits for them, and re-layouts  3.35 us (4%)
    pallas_call x1, Pallas kernels, run_kernel(): pl.pallas_call(kernel, out_shape=(jax.ShapeDtypeStruct(travelling, BF16),...  77.1 us
    unnamed x8, local copies, waits for them, and re-layouts  3.35 us

profile of v2, /device:TPU:13, one launch (start us, length us, event | category | flops | bytes accessed | tf_op | source)
XLA Modules:
  0.0 81.1 jit_solution(13836905164418055667)
XLA Ops:
  0.6 77.1 %attention_backward.1 = (bf16[64,16,128]{2,1,0:T(8,128)(2,1)}, bf16[128,128]{1,0:T(8,128)(2,1)}, bf16[128,128]{1,0:T(8,128)(2,1)}) custom-call(s32[16]{0:T(128)} %lengths.1, s32[1,128]{1,0:T(1,128)} %order.1, bf16[128,768]{1,0:T(8,128)(2,1)} %queries.1, bf16[128,768]{1,0:T(8,128)(2,1)} %cotangent.1, bf16[128,128]{1,0:T(8,128)(2,1)} %keys.1, ...), custom_call_target="tpu_custom_call" | custom-call | tf_op jit(solution)/shard_map/attention_backward/pallas_call | solution.py:484
  77.7 1.1 %copy.11 = bf16[128,6,128]{0,2,1:T(8,128)(2,1)S(1)} copy(bf16[128,6,128]{2,1,0:T(8,128)(2,1)} %bitcast.4) | data formatting | bytes 393216
  78.9 0.0 copy-start.1
  78.9 0.8 %copy.10 = bf16[128,768]{1,0:T(8,128)(2,1)} copy(bf16[128,768]{0,1:T(8,128)(2,1)S(1)} %bitcast.3) | data formatting | bytes 393216
  79.7 0.0 copy-done.1
  79.7 0.0 copy-start
  79.7 0.6 copy.14
  80.3 0.2 copy-done
  80.5 0.6 copy.15
Async XLA Ops:
  78.9 0.8 %copy-start.1 = (bf16[128,128]{1,0:T(8,128)(2,1)S(1)}, bf16[128,128]{1,0:T(8,128)(2,1)}, u32[]{:S(2)}) copy-start(bf16[128,128]{1,0:T(8,128)(2,1)} %get-tuple-element.16) | copy-start | bytes 98308
  79.7 0.8 copy-start

commit v3 on v2

v3 whole, which is shorter than its diff:
```python
import functools
import math

import jax
import jax.numpy as jnp
from jax import lax
from jax.experimental import pallas as pl
from jax.experimental.pallas import tpu as pltpu
from jax.sharding import PartitionSpec as P

HEAD_SIZE = 128
SOFTCAP = 30
TOK = 128
ROWS_Y = 4
RING = 8
SLOTS = 3 * RING
SUM_ROWS = 16
HELD = 17
PAD = 8
GATHER_ORDER = (
    (0, 0), (1, 0), (0, 2), (2, 0), (1, 2), (0, 1), (2, 2), (1, 1), (2, 1), (0, 3), (1, 3), (0, 4), (1, 4), (2, 3), (2, 4)
)
REDUCE_ORDER = (
    (2, 4), (2, 3), (1, 4), (1, 3), (0, 4), (0, 3), (2, 1), (1, 1), (2, 2), (1, 2), (0, 1), (2, 0), (0, 2), (1, 0), (0, 0)
)
PORT = {1: 0, 2: 1, -1: 2, -2: 3, 3: 4, 4: 5, -3: 6, -4: 7}
MESH = pl.DeviceIdType.MESH
F32 = jnp.float32
BF16 = jnp.bfloat16


def dot(a, b, contract=((1,), (0,))):
    return lax.dot_general(a, b, (contract, ((), ())), preferred_element_type=F32)


def send(src, dst, send_sem, recv_sem, target):
    return pltpu.make_async_remote_copy(
        src_ref=src,
        dst_ref=dst,
        send_sem=send_sem,
        recv_sem=recv_sem,
        device_id={"ctx": target},
        device_id_type=MESH,
    )


def needed(row, origin, z):
    return (row == 1) | ((row == 0) & (origin <= z)) | ((row == 2) & (origin >= z))


def reaches(row, origin, shift, core):
    z = lax.rem(origin + shift + RING, RING)
    if abs(shift) == 4:
        if row == 1:
            return core == (0 if shift > 0 else 1)
        return needed(row, origin, z) & ((row == 0) == (shift > 0))
    wanted = needed(row, origin, z)
    if abs(shift) == 2:
        for further in (3, 4):
            wanted = wanted | reaches(row, origin, further if shift > 0 else -further, core)
    return wanted


def pick(index, table):
    value = jnp.int32(table[0])
    for i in range(1, len(table)):
        value = jnp.where(index == i, table[i], value)
    return value


def kernel(
    lengths,
    order,
    queries,
    cotangent,
    keys,
    values,
    dq_out,
    dk_out,
    dv_out,
    kv,
    exps,
    slopes,
    q_t,
    d_t,
    q_rows,
    d_rows,
    q_mate,
    d_mate,
    out_acc,
    dq_acc,
    dq_mate,
    low_slope,
    low_prob,
    stats_out,
    stats_in,
    inverse,
    row_dots,
    bounds,
    spread,
    part,
    ring_out,
    ring_in,
    y_in,
    rows_out,
    rows_in,
    g_ring_send,
    g_ring_recv,
    g_y_send,
    g_y_recv,
    r_ring_send,
    r_ring_recv,
    r_y_send,
    r_y_recv,
    mate_send,
    mate_recv,
    rows_send,
    rows_recv,
    ready,
):
    lanes = queries.shape[1]
    heads = lanes // HEAD_SIZE
    devices = 2 * RING * ROWS_Y
    index = lax.axis_index("ctx")
    core = lax.rem(index, 2)
    z = lax.rem(lax.div(index, 2), RING)
    h = lax.div(index, 2 * RING)
    sibling = index + 1 - 2 * core
    scale = 1.0 / math.sqrt(HEAD_SIZE)

    def along(place):
        return 2 * RING * h + 2 * lax.rem(place + RING, RING) + core

    barrier = pltpu.get_barrier_semaphore()
    ring_mates = [along(z + step) for step in range(1, RING)]
    column_mates = [
        lax.rem(index - core + 2 * RING * step + lax.rem(core + side, 2), devices)
        for step in range(ROWS_Y)
        for side in (0, 1)
        if step or side
    ]
    for mate in ring_mates + column_mates:
        pl.semaphore_signal(barrier, inc=1, device_id={"ctx": mate}, device_id_type=MESH)

    kv[z, 0] = keys[...]
    kv[z, 1] = values[...]
    pl.semaphore_wait(barrier, len(ring_mates + column_mates))

    def gather_ring(row, origin, shift):
        unit = kv.at[row * RING + origin]
        return send(
            unit,
            unit,
            g_ring_send.at[row, PORT[shift]],
            g_ring_recv.at[row * RING + origin],
            along(origin + shift),
        )

    def to_mate(src, dst, which):
        return send(src, dst, mate_send.at[which], mate_recv.at[which], sibling)

    queries_to_mate = to_mate(queries, q_mate, 0)
    cotangent_to_mate = to_mate(cotangent, d_mate, 1)
    stats_to_mate = to_mate(stats_out, stats_in, 2)
    grads_to_mate = to_mate(dq_acc.at[:, pl.ds(lanes, lanes)], dq_mate, 3)

    def gather_y(step):
        return send(
            kv.at[z],
            kv.at[step * RING + z],
            g_y_send.at[step - 1],
            g_y_recv.at[step - 1],
            lax.rem(index + step * 2 * RING, devices),
        )

    def reduce_ring(row, origin, shift):
        stop = 0 if abs(shift) <= 2 else (2 if shift > 0 else -2)
        return send(
            ring_out.at[row * RING + origin],
            ring_in.at[row, PORT[shift]],
            r_ring_send.at[row * RING + origin],
            r_ring_recv.at[row, PORT[shift]],
            along(origin + stop),
        )

    def reduce_y(step):
        return send(
            ring_out.at[step * RING + z],
            y_in.at[step - 1],
            r_y_send.at[step - 1],
            r_y_recv.at[step - 1],
            lax.rem(index + (ROWS_Y - step) * 2 * RING, devices),
        )

    @pl.when(h + 1 < ROWS_Y)
    def _():
        gather_y(1).start()

    def origin_of(shift):
        return lax.rem(z - shift + RING, RING)

    def further_of(shift):
        if abs(shift) != 2:
            return ()
        return (3, 4) if shift > 0 else (-3, -4)

    def arrive(row, distance):
        if distance == 0:
            if row:
                gather_y(row).wait_recv()
            for shift in (2, -2, 1, -1):

                @pl.when(reaches(row, z, shift, core))
                def _():
                    gather_ring(row, z, shift).start()

            return
        for shift in (distance, -distance):
            origin = origin_of(shift)

            @pl.when(reaches(row, origin, shift, core))
            def _():
                gather_ring(row, origin, shift).wait_recv()
                for further in further_of(shift):

                    @pl.when(reaches(row, origin, further, core))
                    def _():
                        gather_ring(row, origin, further).start()

    arrive(*GATHER_ORDER[0])
    queries_to_mate.start()
    cotangent_to_mate.start()

    @pl.when(h + 1 < ROWS_Y)
    def _():
        gather_y(1).wait_send()

    @pl.when(h + 2 < ROWS_Y)
    def _():
        gather_y(2).start()

    for mate in column_mates:
        pl.semaphore_signal(ready, inc=1, device_id={"ctx": mate}, device_id_type=MESH)

    def lay_out(first, rows_q, rows_d):
        for n in range(heads):
            cols = slice(n * HEAD_SIZE, (n + 1) * HEAD_SIZE)
            to = slice(first + n * HEAD_SIZE, first + (n + 1) * HEAD_SIZE)
            q_t[:, to] = rows_q[:, cols].astype(F32).T.astype(BF16)
            d_t[:, to] = rows_d[:, cols].astype(F32).T.astype(BF16)
            q_rows[to, :] = rows_q[:, cols]
            d_rows[to, :] = rows_d[:, cols]

    lay_out(0, queries, cotangent)
    out_acc[...] = jnp.zeros_like(out_acc)
    dq_acc[...] = jnp.zeros_like(dq_acc)
    lane = lax.broadcasted_iota(jnp.int32, (8, TOK), 1)
    position = jnp.concatenate([index * TOK + lane, sibling * TOK + lane], axis=1)
    start = jnp.zeros((8, 2 * TOK), jnp.int32)
    first = jnp.int32(0)
    for doc in range(lengths.shape[0]):
        start = jnp.where(position >= first, jnp.maximum(start, first), start)
        first = first + lengths[doc]
    bounds[0] = start
    bounds[1] = position
    queries_to_mate.wait_recv()
    cotangent_to_mate.wait_recv()
    lay_out(lanes, q_mate, d_mate)

    def member(row, distance, i):
        origin = lax.rem(z + RING + (2 * i - 1) * distance, RING)
        valid = (h >= row) & needed(row, origin, z) & ((i == 0) | ((distance != 0) & (distance != 4)))
        kept = jnp.where(row == 1, RING + origin, jnp.where((row == 2) & (origin == z), 2 * RING, origin))
        return origin, row * RING + origin, kept, valid

    def statistics(row, origin, slot, kept):
        value_t = jnp.concatenate(
            [kv[slot, 1].astype(F32).T.astype(BF16), jnp.ones((SUM_ROWS, TOK), BF16)], axis=0
        )
        key_first = (((h - row) * RING + origin) * 2 + core) * TOK
        key_at = key_first + lax.broadcasted_iota(jnp.int32, (TOK, 2 * TOK), 0)
        visible = (key_at >= bounds[0, :1]) & (key_at <= bounds[1, :1])
        seen = jnp.concatenate([visible[:, :TOK]] * heads + [visible[:, TOK:]] * heads, axis=1)
        bent = jnp.tanh(dot(kv[slot, 0], q_t[...]) * (scale / SOFTCAP))
        weight = jnp.where(seen, jnp.exp2(bent * (SOFTCAP * math.log2(math.e))), 0.0)
        exps[kept] = weight
        slopes[kept] = weight - weight * bent * bent
        out_acc[...] += dot(value_t, weight.astype(BF16))

    def gather_step(g, carry):
        for i in range(1, len(GATHER_ORDER)):

            @pl.when((g == i) & (h >= GATHER_ORDER[i][0]))
            def _():
                arrive(*GATHER_ORDER[i])

        row = pick(g - 1, [r for r, _ in GATHER_ORDER])
        distance = pick(g - 1, [d for _, d in GATHER_ORDER])

        def one(i, carry):
            origin, slot, kept, valid = member(row, distance, i)

            @pl.when(valid)
            def _():
                statistics(row, origin, slot, kept)

            return carry

        return lax.fori_loop(0, 2, one, carry)

    lax.fori_loop(1, len(GATHER_ORDER) + 1, gather_step, 0)

    dots = jnp.sum(out_acc[:HEAD_SIZE, :] * d_t[...].astype(F32), axis=0, keepdims=True)
    stats_out[0] = out_acc[HEAD_SIZE : HEAD_SIZE + 8, :]
    stats_out[1] = jnp.broadcast_to(dots, (8, 2 * lanes))
    stats_to_mate.start()

    picked = (lax.broadcasted_iota(jnp.int32, (TOK, TOK), 0) == order[...]).astype(F32).T.astype(BF16)
    target = lax.broadcasted_iota(jnp.int32, (TOK * PAD, TOK), 0)
    source = PAD * lax.broadcasted_iota(jnp.int32, (TOK * PAD, TOK), 1)
    for n in range(heads):
        place = (target == source + n).astype(F32).astype(BF16)
        spread[:, n * HEAD_SIZE : (n + 1) * HEAD_SIZE] = dot(place, picked).astype(BF16)

    stats_to_mate.wait_recv()
    mine, other = slice(0, lanes), slice(lanes, 2 * lanes)
    for here, there in ((mine, other), (other, mine)):
        inverse_sum = 1.0 / (stats_out[0, :, here] + stats_in[0, :, there])
        inverse[:, here] = inverse_sum
        row_dots[:, here] = (stats_out[1, :, here] + stats_in[1, :, there]) * inverse_sum

    def gradients(slot, kept):
        key_t = kv[slot, 0].astype(F32).T.astype(BF16)
        inv = inverse[:1, :]
        dots = (dot(kv[slot, 1], d_t[...]) - row_dots[:1, :]) * inv
        slope = (slopes[kept] * dots).astype(BF16)
        low_slope[...] = slope
        low_prob[...] = (exps[kept] * inv).astype(BF16)
        dq_acc[...] += dot(key_t, slope)
        part[slot, 0] = dot(low_slope[...], q_rows[...])
        part[slot, 1] = dot(low_prob[...], d_rows[...])

    def combine(row, distance):
        if distance == 0:
            slot = row * RING + z
            for shift in (1, -1, 2, -2):

                @pl.when(reaches(row, z, shift, core))
                def _():
                    reduce_ring(row, z, shift).wait_recv()
                    part[slot] = part[slot] + ring_in[row, PORT[shift]].astype(F32)

            if row:
                ring_out[slot] = part[slot].astype(BF16)
                reduce_y(row).start()
            return
        for shift in (distance, -distance):
            origin = origin_of(shift)
            slot = row * RING + origin

            @pl.when(reaches(row, origin, shift, core))
            def _():
                if distance == 2:

                    @pl.when(jnp.logical_not(needed(row, origin, z)))
                    def _():
                        part[slot] = jnp.zeros(part.shape[1:], F32)

                for further in further_of(shift):

                    @pl.when(reaches(row, origin, further, core))
                    def _():
                        reduce_ring(row, origin, further).wait_recv()
                        part[slot] = part[slot] + ring_in[row, PORT[further]].astype(F32)

                ring_out[slot] = part[slot].astype(BF16)
                reduce_ring(row, origin, shift).start()

    def reduce_step(g, carry):
        row = pick(g, [r for r, _ in REDUCE_ORDER])
        distance = pick(g, [d for _, d in REDUCE_ORDER])

        def one(i, carry):
            _, slot, kept, valid = member(row, distance, i)

            @pl.when(valid)
            def _():
                gradients(slot, kept)

            return carry

        carry = lax.fori_loop(0, 2, one, carry)
        for i, (row_at, distance_at) in enumerate(REDUCE_ORDER):
            if distance_at:

                @pl.when((g == i) & (h >= row_at))
                def _():
                    combine(row_at, distance_at)

        return carry

    lax.fori_loop(0, len(REDUCE_ORDER), reduce_step, 0)

    grads_to_mate.start()
    grads_to_mate.wait_recv()
    grad_t = ((dq_acc[:, mine] + dq_mate[...]) * scale).astype(BF16)
    moved = dot(spread[...], grad_t, ((1,), (1,))).astype(BF16)
    rows_out[...] = moved.reshape(rows_out.shape)

    pl.semaphore_wait(ready, len(column_mates))

    def rows_to(step, carry):
        owner = lax.rem(index + step, devices)
        send(rows_out.at[owner], rows_in.at[index], rows_send, rows_recv, owner).start()
        return carry

    lax.fori_loop(1, devices, rows_to, 0)
    rows_in[index] = rows_out[index]

    for row in (2, 1, 0):

        @pl.when(h >= row)
        def _():
            combine(row, 0)

    for step in (1, 2):

        @pl.when(h + step < ROWS_Y)
        def _():
            reduce_y(step).wait_recv()
            part[z] = part[z] + y_in[step - 1].astype(F32)

    dk_out[...] = (part[z, 0] * scale).astype(BF16)
    dv_out[...] = part[z, 1].astype(BF16)

    @pl.when(h + 2 < ROWS_Y)
    def _():
        gather_y(2).wait_send()

    for step in (1, 2):

        @pl.when(h >= step)
        def _():
            reduce_y(step).wait_send()

    for row in range(3):

        @pl.when(h >= row)
        def _():
            for shift in PORT:
                origin = origin_of(shift)
                if abs(shift) <= 2:

                    @pl.when(reaches(row, z, shift, core))
                    def _():
                        gather_ring(row, z, shift).wait_send()

                for further in further_of(shift):

                    @pl.when(reaches(row, origin, further, core))
                    def _():
                        gather_ring(row, origin, further).wait_send()

                @pl.when(reaches(row, origin, shift, core))
                def _():
                    reduce_ring(row, origin, shift).wait_send()

    for copy in (queries_to_mate, cotangent_to_mate, stats_to_mate, grads_to_mate):
        copy.wait_send()
    others = pl.ds(0, devices - 1)
    everyone = send(rows_out.at[others], rows_in.at[others], rows_send, rows_recv, sibling)
    everyone.wait_recv()
    everyone.wait_send()
    dq_out[...] = rows_in[...]


def run_kernel(queries, cotangent, keys, values, lengths, order):
    lanes = queries.shape[1]
    devices = lax.axis_size("ctx")
    vmem = pl.BlockSpec(memory_space=pltpu.VMEM)
    block = (2, TOK, HEAD_SIZE)
    travelling = (devices, TOK // devices * PAD, HEAD_SIZE)
    dma = pltpu.SemaphoreType.DMA
    return pl.pallas_call(
        kernel,
        out_shape=(
            jax.ShapeDtypeStruct(travelling, BF16),
            jax.ShapeDtypeStruct((TOK, HEAD_SIZE), BF16),
            jax.ShapeDtypeStruct((TOK, HEAD_SIZE), BF16),
        ),
        in_specs=[pl.BlockSpec(memory_space=pltpu.SMEM)] + [vmem] * 5,
        out_specs=(vmem, vmem, vmem),
        scratch_shapes=[
            pltpu.VMEM((SLOTS,) + block, BF16),
            pltpu.VMEM((HELD, TOK, 2 * lanes), F32),
            pltpu.VMEM((HELD, TOK, 2 * lanes), F32),
            pltpu.VMEM((HEAD_SIZE, 2 * lanes), BF16),
            pltpu.VMEM((HEAD_SIZE, 2 * lanes), BF16),
            pltpu.VMEM((2 * lanes, HEAD_SIZE), BF16),
            pltpu.VMEM((2 * lanes, HEAD_SIZE), BF16),
            pltpu.VMEM((TOK, lanes), BF16),
            pltpu.VMEM((TOK, lanes), BF16),
            pltpu.VMEM((HEAD_SIZE + SUM_ROWS, 2 * lanes), F32),
            pltpu.VMEM((HEAD_SIZE, 2 * lanes), F32),
            pltpu.VMEM((HEAD_SIZE, lanes), F32),
            pltpu.VMEM((TOK, 2 * lanes), BF16),
            pltpu.VMEM((TOK, 2 * lanes), BF16),
            pltpu.VMEM((2, 8, 2 * lanes), F32),
            pltpu.VMEM((2, 8, 2 * lanes), F32),
            pltpu.VMEM((8, 2 * lanes), F32),
            pltpu.VMEM((8, 2 * lanes), F32),
            pltpu.VMEM((2, 8, 2 * TOK), jnp.int32),
            pltpu.VMEM((TOK * PAD, lanes), BF16),
            pltpu.VMEM((SLOTS,) + block, F32),
            pltpu.VMEM((SLOTS,) + block, BF16),
            pltpu.VMEM((3, len(PORT)) + block, BF16),
            pltpu.VMEM((2,) + block, BF16),
            pltpu.VMEM(travelling, BF16),
            pltpu.VMEM(travelling, BF16),
            dma((3, len(PORT))),
            dma((SLOTS,)),
            dma((2,)),
            dma((2,)),
            dma((SLOTS,)),
            dma((3, len(PORT))),
            dma((2,)),
            dma((2,)),
            dma((4,)),
            dma((4,)),
            dma,
            dma,
            pltpu.SemaphoreType.REGULAR,
        ],
        compiler_params=pltpu.CompilerParams(
            collective_id=0, has_side_effects=True, vmem_limit_bytes=58 * 1024 * 1024
        ),
        name="attention_backward",
    )(lengths, order, queries, cotangent, keys, values)


def on_device(queries, keys, values, output_cotangent, lengths, send_order):
    rows, lanes = queries.shape
    moved, dk, dv = run_kernel(queries, output_cotangent, keys, values, lengths, send_order)
    dq_owned = moved.reshape(rows, PAD, HEAD_SIZE)[:, : lanes // HEAD_SIZE]
    return dq_owned.reshape(rows, lanes), dk, dv


def solution(mesh):
    return jax.shard_map(
        on_device,
        mesh=mesh,
        in_specs=(
            P("ctx", "head"),
            P("ctx", "head"),
            P("ctx", "head"),
            P("ctx", "head"),
            P(),
            P("ctx", None),
        ),
        out_specs=(P("ctx", "head"), P("ctx", "head"), P("ctx", "head")),
        check_vma=False,
    )
```

time: 81.3 us -> 79 us (0.972)
  the two profiles are of different devices: /device:TPU:13 before, /device:TPU:21 now
where the time goes in v3:
time: 79 us; the launch traced here: 78.8 us
  Pallas kernels  74.8 us (95%)
  local copies, waits for them, and re-layouts  3.35 us (4%)
    pallas_call x1, Pallas kernels, run_kernel(): pl.pallas_call(kernel, out_shape=(jax.ShapeDtypeStruct(travelling, BF16),...  74.8 us
    unnamed x8, local copies, waits for them, and re-layouts  3.35 us

profile of v3, /device:TPU:21, one launch (start us, length us, event | category | flops | bytes accessed | tf_op | source)
XLA Modules:
  0.0 78.8 jit_solution(12578470948921979027)
XLA Ops:
  0.6 74.8 %attention_backward.1 = (bf16[64,16,128]{2,1,0:T(8,128)(2,1)}, bf16[128,128]{1,0:T(8,128)(2,1)}, bf16[128,128]{1,0:T(8,128)(2,1)}) custom-call(s32[16]{0:T(128)} %lengths.1, s32[1,128]{1,0:T(1,128)} %order.1, bf16[128,768]{1,0:T(8,128)(2,1)} %queries.1, bf16[128,768]{1,0:T(8,128)(2,1)} %cotangent.1, bf16[128,128]{1,0:T(8,128)(2,1)} %keys.1, ...), custom_call_target="tpu_custom_call" | custom-call | tf_op jit(solution)/shard_map/attention_backward/pallas_call | solution.py:484
  75.4 1.1 %copy.11 = bf16[128,6,128]{0,2,1:T(8,128)(2,1)S(1)} copy(bf16[128,6,128]{2,1,0:T(8,128)(2,1)} %bitcast.4) | data formatting | bytes 393216
  76.6 0.0 copy-start.1
  76.6 0.8 %copy.10 = bf16[128,768]{1,0:T(8,128)(2,1)} copy(bf16[128,768]{0,1:T(8,128)(2,1)S(1)} %bitcast.3) | data formatting | bytes 393216
  77.4 0.0 copy-done.1
  77.4 0.0 copy-start
  77.4 0.6 copy.14
  78.0 0.2 copy-done
  78.2 0.6 copy.15
Async XLA Ops:
  76.6 0.8 %copy-start.1 = (bf16[128,128]{1,0:T(8,128)(2,1)S(1)}, bf16[128,128]{1,0:T(8,128)(2,1)}, u32[]{:S(2)}) copy-start(bf16[128,128]{1,0:T(8,128)(2,1)} %get-tuple-element.16) | copy-start | bytes 98308
  77.4 0.8 copy-start

commit v4 on v3

--- a/solution.py
+++ b/solution.py
@@ -21,7 +21,7 @@
     (0, 0), (1, 0), (0, 2), (2, 0), (1, 2), (0, 1), (2, 2), (1, 1), (2, 1), (0, 3), (1, 3), (0, 4), (1, 4), (2, 3), (2, 4)
 )
 REDUCE_ORDER = (
-    (2, 4), (2, 3), (1, 4), (1, 3), (0, 4), (0, 3), (2, 1), (1, 1), (2, 2), (1, 2), (0, 1), (2, 0), (0, 2), (1, 0), (0, 0)
+    (2, 4), (2, 3), (1, 4), (1, 3), (2, 1), (0, 4), (0, 3), (1, 1), (0, 1), (2, 2), (1, 2), (0, 2), (2, 0), (1, 0), (0, 0)
 )
 PORT = {1: 0, 2: 1, -1: 2, -2: 3, 3: 4, 4: 5, -3: 6, -4: 7}
 MESH = pl.DeviceIdType.MESH
@@ -402,6 +402,12 @@
     lax.fori_loop(0, len(REDUCE_ORDER), reduce_step, 0)
 
     grads_to_mate.start()
+    for row in (2,):
+
+        @pl.when(h >= row)
+        def _():
+            combine(row, 0)
+
     grads_to_mate.wait_recv()
     grad_t = ((dq_acc[:, mine] + dq_mate[...]) * scale).astype(BF16)
     moved = dot(spread[...], grad_t, ((1,), (1,))).astype(BF16)
@@ -417,7 +423,7 @@
     lax.fori_loop(1, devices, rows_to, 0)
     rows_in[index] = rows_out[index]
 
-    for row in (2, 1, 0):
+    for row in (1, 0):
 
         @pl.when(h >= row)
         def _():

time: 79 us -> 77.4 us (0.980)
  the two profiles are of different devices: /device:TPU:21 before, /device:TPU:6 now
where the time goes in v4:
time: 77.4 us; the launch traced here: 76.1 us
  Pallas kernels  72.1 us (93%)
  local copies, waits for them, and re-layouts  3.35 us (4%)
    pallas_call x1, Pallas kernels, run_kernel(): pl.pallas_call(kernel, out_shape=(jax.ShapeDtypeStruct(travelling, BF16),...  72.1 us
    unnamed x8, local copies, waits for them, and re-layouts  3.35 us

profile of v4, /device:TPU:6, one launch (start us, length us, event | category | flops | bytes accessed | tf_op | source)
XLA Modules:
  0.0 76.1 jit_solution(4600294566491331708)
XLA Ops:
  0.6 72.1 %attention_backward.1 = (bf16[64,16,128]{2,1,0:T(8,128)(2,1)}, bf16[128,128]{1,0:T(8,128)(2,1)}, bf16[128,128]{1,0:T(8,128)(2,1)}) custom-call(s32[16]{0:T(128)} %lengths.1, s32[1,128]{1,0:T(1,128)} %order.1, bf16[128,768]{1,0:T(8,128)(2,1)} %queries.1, bf16[128,768]{1,0:T(8,128)(2,1)} %cotangent.1, bf16[128,128]{1,0:T(8,128)(2,1)} %keys.1, ...), custom_call_target="tpu_custom_call" | custom-call | tf_op jit(solution)/shard_map/attention_backward/pallas_call | solution.py:490
  72.7 1.1 %copy.11 = bf16[128,6,128]{0,2,1:T(8,128)(2,1)S(1)} copy(bf16[128,6,128]{2,1,0:T(8,128)(2,1)} %bitcast.4) | data formatting | bytes 393216
  73.8 0.0 copy-start.1
  73.8 0.8 %copy.10 = bf16[128,768]{1,0:T(8,128)(2,1)} copy(bf16[128,768]{0,1:T(8,128)(2,1)S(1)} %bitcast.3) | data formatting | bytes 393216
  74.7 0.0 copy-done.1
  74.7 0.0 copy-start
  74.7 0.6 copy.14
  75.3 0.2 copy-done
  75.4 0.6 copy.15
Async XLA Ops:
  73.8 0.8 %copy-start.1 = (bf16[128,128]{1,0:T(8,128)(2,1)S(1)}, bf16[128,128]{1,0:T(8,128)(2,1)}, u32[]{:S(2)}) copy-start(bf16[128,128]{1,0:T(8,128)(2,1)} %get-tuple-element.16) | copy-start | bytes 98308
  74.7 0.8 %copy-start = (bf16[128,128]{1,0:T(8,128)(2,1)S(1)}, bf16[128,128]{1,0:T(8,128)(2,1)}, u32[]{:S(2)}) copy-start(bf16[128,128]{1,0:T(8,128)(2,1)} %get-tuple-element.17) | copy-start | bytes 98308

commit v5 on v4

--- a/solution.py
+++ b/solution.py
@@ -547,8 +547,8 @@
 def on_device(queries, keys, values, output_cotangent, lengths, send_order):
     rows, lanes = queries.shape
     moved, dk, dv = run_kernel(queries, output_cotangent, keys, values, lengths, send_order)
-    dq_owned = moved.reshape(rows, PAD, HEAD_SIZE)[:, : lanes // HEAD_SIZE]
-    return dq_owned.reshape(rows, lanes), dk, dv
+    padded = moved.reshape(rows, PAD * HEAD_SIZE)
+    return padded[:, :lanes], dk, dv
 
 
 def solution(mesh):

time: 77.4 us -> 77.3 us (level)
    unnamed x8 -> x6, local copies, waits for them, and re-layouts: 3.35 us -> 1.44 us
    reshape x0 -> x1, local copies, waits for them, and re-layouts: none -> 1.07 us  [on_device(): padded = moved.reshape(rows, PAD * HEAD_SIZE)]
where the time goes in v5:
time: 77.3 us; the launch traced here: 75.9 us
  Pallas kernels  72.1 us (93%)
  local copies, waits for them, and re-layouts  3.2 us (4%)
    pallas_call x1, Pallas kernels, run_kernel(): pl.pallas_call(kernel, out_shape=(jax.ShapeDtypeStruct(travelling, BF16),...  72.1 us

profile of v5, /device:TPU:6, one launch (start us, length us, event | category | flops | bytes accessed | tf_op | source)
XLA Modules:
  0.0 75.9 jit_solution(10850437801157435036)
XLA Ops:
  0.6 72.1 %attention_backward.1 = (bf16[64,16,128]{2,1,0:T(8,128)(2,1)}, bf16[128,128]{1,0:T(8,128)(2,1)}, bf16[128,128]{1,0:T(8,128)(2,1)}) custom-call(s32[16]{0:T(128)} %lengths.1, s32[1,128]{1,0:T(1,128)} %order.1, bf16[128,768]{1,0:T(8,128)(2,1)} %queries.1, bf16[128,768]{1,0:T(8,128)(2,1)} %cotangent.1, bf16[128,128]{1,0:T(8,128)(2,1)} %keys.1, ...), custom_call_target="tpu_custom_call" | custom-call | tf_op jit(solution)/shard_map/attention_backward/pallas_call | solution.py:490
  72.7 1.1 %reshape.9 = bf16[128,1024]{1,0:T(8,128)(2,1)S(1)} reshape(bf16[64,16,128]{2,1,0:T(8,128)(2,1)} %get-tuple-element.6) | data formatting | bytes 524288 | tf_op jit(solution)/shard_map/reshape | solution.py:550
  73.8 0.0 copy-start.1
  73.8 0.7 slice.4
  74.5 0.1 copy-done.1
  74.5 0.0 copy-start
  74.5 0.6 copy.11
  75.1 0.2 copy-done
  75.3 0.6 copy.12
Async XLA Ops:
  73.8 0.8 copy-start.1
  74.5 0.8 %copy-start = (bf16[128,128]{1,0:T(8,128)(2,1)S(1)}, bf16[128,128]{1,0:T(8,128)(2,1)}, u32[]{:S(2)}) copy-start(bf16[128,128]{1,0:T(8,128)(2,1)} %get-tuple-element.14) | copy-start | bytes 98308
